TPU v7x, 32 devices: a whole 2x2x4 slice. The times are simulated.
32 devices in a mesh: ty: 4 (over x, core), tx: 8 (over z, y).
Axes of the slice: x: 2, y: 2, z: 4, core: 2. Of those that a mesh axis runs over, the one named last changes fastest.
Arguments:
- gaussians: float32 [3072, 59, 128], P(('ty', 'tx')), may hold values from -14 to 18, as said below
- tile_lists: int32 [4, 8, 24], P('ty', 'tx'), may hold values from 0 to 3071, as said below
- tile_counts: int32 [4, 8], P('ty', 'tx'), may hold values from 3 to 24, as said below
- depth_order: int32 [3072], replicated, may hold values from 0 to 3071, as said below
- target: float32 [3, 128, 256], P(None, 'ty', 'tx'), may hold values from 0 to 1
Outputs:
- gaussian_grads: float32 [3072, 59, 128], P(('ty', 'tx'))
- loss: float32 [], replicated
Inputs may be any that keep to these rules, and one draw needn't show every extreme that they name: `tile_lists`: entries beyond a tile's count are arbitrary ranks. The live entries of a tile are rising depth ranks of blocks owned by devices in the tile's own row of ty (block b belongs to device b // 96 of ty+tx, ty slowest). At most 3 live entries of one tile name blocks of one owner; in every row some owner is named 3 times by every tile of the row. No block is live in two entries. `tile_counts`: some tile has 24 in every draw. A permutation: depth_order[r] is the block at depth rank r. `gaussians`: row 2 (Z) lies between 1.5 and 12, row 6 (the quaternion's w) between 0.5 and 1.5.
All inputs are finite; a program needn't handle non-finite values.
Results may differ from a plain program's by a relative error of at most 0.0003.
Values sent between devices are 32-bit elements; how exact they have to be, the bound alone decides.
No kernel may reach another device: no remote copies, remote signals or barrier semaphores. Data moves between devices by JAX's collectives and lax.ppermute only.
A program may use at most 64 MiB of HBM per device.

v0:
```python
import functools

import jax
import jax.numpy as jnp
import ml_dtypes
import numpy as np
from jax import lax
from jax.experimental import pallas as pl
from jax.experimental.pallas import tpu as pltpu
from jax.sharding import PartitionSpec as P

CAP = 3
SEGS = 8
LANES = 128
CHUNK = 256
STEPS = CHUNK // SEGS
SPAN = 4
COLS = 256
RIM = 5
TAPS = 2 * RIM + 1
LOG2E = 1.4426950408889634
LN2 = 0.6931471805599453
DARK = -1e30

FOCAL = 1000.0
LOW_PASS = 0.3
STRUCT_WEIGHT = 0.2
LUMA_TERM = 0.0001
CONTRAST_TERM = 0.0009
ROBUST_TERM = 1e-06
HARMONIC_ZERO = 0.28209479177387814
HARMONIC_ONE = 0.4886025119029199
HARMONIC_TWO = (
    1.0925484305920792,
    -1.0925484305920792,
    0.31539156525252005,
    -1.0925484305920792,
    0.5462742152960396,
)
HARMONIC_THREE = (
    -0.5900435899266435,
    2.890611442640554,
    -0.4570457994644658,
    0.3731763325901154,
    -0.4570457994644658,
    1.445305721320277,
    -0.5900435899266435,
)

HIGH = lax.Precision.HIGHEST
F32 = jnp.float32
BF16 = jnp.bfloat16
ANY = pl.BlockSpec(memory_space=pl.ANY)
SMEM = pl.BlockSpec(memory_space=pltpu.SMEM)
VMEM = pl.BlockSpec(memory_space=pltpu.VMEM)
PARAMS = pltpu.CompilerParams(vmem_limit_bytes=24 * 1024 * 1024)


def harmonics(x, y, z):
    xx, yy, zz = x * x, y * y, z * z
    xy, yz, xz = x * y, y * z, x * z
    return [
        HARMONIC_ZERO * jnp.ones_like(x),
        -HARMONIC_ONE * y,
        HARMONIC_ONE * z,
        -HARMONIC_ONE * x,
        HARMONIC_TWO[0] * xy,
        HARMONIC_TWO[1] * yz,
        HARMONIC_TWO[2] * (2.0 * zz - xx - yy),
        HARMONIC_TWO[3] * xz,
        HARMONIC_TWO[4] * (xx - yy),
        HARMONIC_THREE[0] * y * (3.0 * xx - yy),
        HARMONIC_THREE[1] * xy * z,
        HARMONIC_THREE[2] * y * (4.0 * zz - xx - yy),
        HARMONIC_THREE[3] * z * (2.0 * zz - 3.0 * xx - 3.0 * yy),
        HARMONIC_THREE[4] * x * (4.0 * zz - xx - yy),
        HARMONIC_THREE[5] * z * (xx - yy),
        HARMONIC_THREE[6] * x * (xx - 3.0 * yy),
    ]


def directions(x, y, z):
    length = jnp.sqrt(x * x + y * y + z * z)
    return harmonics(x / length, y / length, z / length)


def conic(mean_x, mean_y, mean_z, log_scale, quat):
    scale = [jnp.exp(s) for s in log_scale]
    norm = jnp.sqrt(quat[0] * quat[0] + quat[1] * quat[1] + quat[2] * quat[2] + quat[3] * quat[3])
    w, i, j, k = (q / norm for q in quat)
    rotation = [
        [1.0 - 2.0 * (j * j + k * k), 2.0 * (i * j - w * k), 2.0 * (i * k + w * j)],
        [2.0 * (i * j + w * k), 1.0 - 2.0 * (i * i + k * k), 2.0 * (j * k - w * i)],
        [2.0 * (i * k - w * j), 2.0 * (j * k + w * i), 1.0 - 2.0 * (i * i + j * j)],
    ]
    scaled = [[rotation[r][c] * scale[c] for c in range(3)] for r in range(3)]

    def sigma(r, c):
        return scaled[r][0] * scaled[c][0] + scaled[r][1] * scaled[c][1] + scaled[r][2] * scaled[c][2]

    s00, s01, s02, s11, s12, s22 = (
        sigma(0, 0), sigma(0, 1), sigma(0, 2), sigma(1, 1), sigma(1, 2), sigma(2, 2),
    )
    inverse_z = 1.0 / mean_z
    diag = FOCAL * inverse_z
    jac_xz = -FOCAL * mean_x * inverse_z * inverse_z
    jac_yz = -FOCAL * mean_y * inverse_z * inverse_z
    u0, u1, u2 = diag * s00 + jac_xz * s02, diag * s01 + jac_xz * s12, diag * s02 + jac_xz * s22
    v1, v2 = diag * s11 + jac_yz * s12, diag * s12 + jac_yz * s22
    cov_uu = u0 * diag + u2 * jac_xz + LOW_PASS
    cov_uv = u1 * diag + u2 * jac_yz
    cov_vv = v1 * diag + v2 * jac_yz + LOW_PASS
    determinant = cov_uu * cov_vv - cov_uv * cov_uv
    half = -0.5 * LOG2E
    xx = half * (cov_vv / determinant)
    xy = (-2.0 * half) * (cov_uv / determinant)
    yy = half * (cov_uu / determinant)
    return xx, xy, yy, FOCAL * mean_x * inverse_z, FOCAL * mean_y * inverse_z


def expanded(xx, xy, yy, pos_u, pos_v, log_opacity):
    x1 = -2.0 * xx * pos_u - xy * pos_v
    y1 = -2.0 * yy * pos_v - xy * pos_u
    one = xx * pos_u * pos_u + xy * pos_u * pos_v + yy * pos_v * pos_v + log_opacity
    return xx, xy, yy, x1, y1, one


def tile_shifts(across, side, height, width):
    column = lax.broadcasted_iota(jnp.int32, (across, LANES), 0).astype(F32)
    column = jnp.concatenate([column] * CAP, axis=0)
    row = lax.axis_index("ty").astype(F32)
    shift_x = (0.5 * width - 0.5 * side - 0.5) - side * column
    shift_y = jnp.full(column.shape, (0.5 * height - 0.5 * side - 0.5) - side * row, F32)
    return shift_x, shift_y


def request_kernel(owned, across, lists, count, order, request, slot, seen):
    base = lax.axis_index("ty") * across
    for o in range(across):
        seen[o] = 0
        for c in range(CAP):
            request[o, 0, c] = -1
    used = count[0, 0]

    def entry(k, _):
        @pl.when(k < used)
        def _():
            block = order[lists[0, 0, k]]
            home = block // owned
            local = block - home * owned
            home = home - base
            at = seen[home]
            seen[home] = at + 1
            request[home, 0, at] = local
            slot[k] = home * CAP + at

        return 0

    lax.fori_loop(0, slot.shape[0], entry, 0, unroll=True)
    free = 0
    for o in range(across):
        free = jnp.where(seen[o] < CAP, o * CAP + CAP - 1, free)

    def rest(k, _):
        slot[k] = free
        return 0

    lax.fori_loop(used, slot.shape[0], rest, 0)


def project_kernel(span, gaussians, out):
    def part(n, _):
        rows = pl.ds(pl.multiple_of(n * span, span), span)
        field = [gaussians[f, rows, :] for f in range(11)]
        light = -LOG2E * jnp.log(1.0 + jnp.exp(-field[10])) + float(np.log2(0.99))
        values = list(conic(field[0], field[1], field[2], field[3:6], field[6:10]))
        values.append(jnp.maximum(light, DARK))
        basis = directions(field[0], field[1], field[2])
        for ch in range(3):
            color = 0.5 + basis[0] * gaussians[11 + ch, rows, :]
            for m in range(1, 16):
                color = color + basis[m] * gaussians[11 + 3 * m + ch, rows, :]
            values.append(color)
        for f in range(9):
            out[f, rows, :] = values[f]
        return 0

    lax.fori_loop(0, gaussians.shape[1] // span, part, 0)


def asked_index(asked, across, s):
    c = s // across
    return asked[s - c * across, 0, c]


def serve_kernel(across, side, height, width, asked, projected, send, chosen):
    def pick(s, _):
        index = jnp.maximum(asked_index(asked, across, s), 0)
        for f in range(9):
            chosen[f, pl.ds(s, 1), :] = projected[f, pl.ds(index, 1), :]
        return 0

    lax.fori_loop(0, across * CAP, pick, 0, unroll=True)
    shift_x, shift_y = tile_shifts(across, side, height, width)
    rows = list(
        expanded(
            chosen[0], chosen[1], chosen[2], chosen[3] + shift_x, chosen[4] + shift_y, chosen[5]
        )
    ) + [chosen[6], chosen[7], chosen[8]]
    for c in range(CAP):
        for f in range(9):
            at = c * 8 + f if f < 8 else CAP * 8 + c
            send[:, at, :] = rows[f][c * across : (c + 1) * across]


def monomials(side):
    pixels = side * side
    lane = lax.broadcasted_iota(jnp.int32, (8, pixels), 1)
    row = lax.broadcasted_iota(jnp.int32, (8, pixels), 0)
    x = ((lane & (side - 1)) - side // 2).astype(F32)
    y = ((lane >> (side.bit_length() - 1)) - side // 2).astype(F32)
    mono = jnp.zeros((8, pixels), F32)
    for at, value in enumerate((x * x, x * y, y * y, x, y, jnp.ones_like(x))):
        mono = jnp.where(row == at, value, mono)
    blank = jnp.zeros((8, pixels), F32)
    rest = jnp.zeros((LANES - 48, pixels), F32)
    return jnp.concatenate([mono, blank] * 3 + [rest], axis=0).astype(BF16)


def spreaders():
    row = lax.broadcasted_iota(jnp.int32, (LANES, LANES), 0)
    return jnp.concatenate(
        [jnp.where((row == 6 + c) | (row == 22 + c), 1.0, 0.0).astype(F32) for c in range(3)], axis=1
    ).astype(BF16)


def repeated(x, times):
    return jnp.concatenate([x] * times, axis=1)


def forward_kernel(
    side, slot, count, recv, target, table, checks, prefix, behind, dense,
    planes, spread, buf_a, buf_b, ends,
):
    lmax = slot.shape[0]
    per = lmax // SEGS
    pixels = prefix.shape[1]
    groups = pixels // LANES
    planes[:, :pixels] = monomials(side)
    planes[:, pixels:] = spreaders()
    zero_rows = jnp.zeros((7, LANES), F32)
    dead = jnp.where(lax.broadcasted_iota(jnp.int32, (16, LANES), 0) == 5, DARK, 0.0)
    is_color = lax.broadcasted_iota(jnp.int32, (16, LANES), 0) >= 6
    filler = jnp.zeros((LANES - 48, LANES), F32)

    def place(m, seg):
        s = slot[seg * per + m]
        live = seg * per + m < count[0, 0]
        o = s // CAP
        c = s - o * CAP
        head = recv[o, pl.ds(pl.multiple_of(c * 8, 8), 8), :]
        tail = recv[o, pl.ds(CAP * 8 + c, 1), :]
        rows = jnp.concatenate([head, tail, zero_rows], axis=0)
        rows = jnp.where(live, rows, dead)
        hi = rows.astype(BF16).astype(F32)
        rest = rows - hi
        mid = rest.astype(BF16).astype(F32)
        low = (rest - mid).astype(BF16).astype(F32)
        third = jnp.where(is_color, hi, low)
        stacked = jnp.concatenate([hi, mid, third, filler], axis=0)
        spread[pl.ds(m * (SEGS * LANES) + seg, LANES, stride=SEGS), :] = stacked.T

    for seg in range(SEGS):
        place(0, seg)

    width = planes.shape[1]
    pieces = -(-width // COLS)

    def product(n, buf, p):
        rows = pl.ds(pl.multiple_of(n * CHUNK, CHUNK), CHUNK)
        if p == 0:
            table[rows, :] = spread[rows, :].astype(BF16)
        cols = slice(p * COLS, min((p + 1) * COLS, width))
        buf[:, cols] = jnp.dot(table[rows, :], planes[:, cols], preferred_element_type=F32)

    def blend(n, b, buf, carry):
        light, red, green, blue = carry
        checks[n * (STEPS // SPAN) + b] = light
        for i in range(b * SPAN, (b + 1) * SPAN):
            rows = pl.ds(i * SEGS, SEGS)
            weight = light * jnp.exp2(buf[rows, :pixels])
            light = light - weight
            red = red + weight * repeated(buf[rows, pixels : pixels + LANES], groups)
            green = green + weight * repeated(buf[rows, pixels + LANES : pixels + 2 * LANES], groups)
            blue = blue + weight * repeated(
                buf[rows, pixels + 2 * LANES : pixels + 3 * LANES], groups
            )
        return light, red, green, blue

    for p in range(pieces):
        product(0, buf_a, p)
    chunks = lmax * LANES // CHUNK
    turn = chunks // per
    share = SEGS // turn

    def pair(h, carry):
        n = 2 * h
        m = (n // turn + 1) % per
        for b in range(STEPS // SPAN):
            if b < pieces:
                product(n + 1, buf_b, b)
            if b % 2 == 0 and b // 2 < 2 * share:
                place(m, (n % turn) * share + b // 2)
            carry = blend(n, b, buf_a, carry)
        for b in range(STEPS // SPAN):
            if b < pieces:
                product(jnp.minimum(n + 2, chunks - 1), buf_a, b)
            carry = blend(n + 1, b, buf_b, carry)
        return carry

    start = (jnp.ones((SEGS, pixels), F32),) + (jnp.zeros((SEGS, pixels), F32),) * 3
    carry = lax.fori_loop(0, chunks // 2, pair, start)
    for f in range(4):
        ends[f] = carry[f]
    ahead = jnp.ones((1, pixels), F32)
    for seg in range(SEGS):
        prefix[pl.ds(seg, 1), :] = ahead
        ahead = ahead * ends[0, pl.ds(seg, 1), :]
    for ch in range(3):
        seen = jnp.zeros((1, pixels), F32)
        for seg in reversed(range(SEGS)):
            behind[ch, pl.ds(seg, 1), :] = seen
            seen = ends[1 + ch, pl.ds(seg, 1), :] + ends[0, pl.ds(seg, 1), :] * seen
        for j in range(groups):
            dense[pl.ds(ch * groups + j, 1), :] = seen[:, j * LANES : (j + 1) * LANES]
    dense[3 * groups :, :] = target[...]


def similarity(mean_a, mean_b, square_a, square_b, cross):
    var_a = square_a - mean_a * mean_a
    var_b = square_b - mean_b * mean_b
    covar = cross - mean_a * mean_b
    top = (2.0 * mean_a * mean_b + LUMA_TERM) * (2.0 * covar + CONTRAST_TERM)
    bottom = (mean_a * mean_a + mean_b * mean_b + LUMA_TERM) * (var_a + var_b + CONTRAST_TERM)
    return top / bottom


def tap(distance):
    weights = [float(np.exp(-((k - RIM) ** 2) / 4.5)) for k in range(TAPS)]
    value = jnp.exp(distance * distance * (-1.0 / 4.5)) * (1.0 / sum(weights))
    return jnp.where(jnp.abs(distance) <= RIM, value, 0.0)


def places(shape, dim):
    return lax.broadcasted_iota(jnp.int32, shape, dim)


def bands(side, padded):
    fold = LANES // side
    groups = side // fold
    reach = side + 2 * RIM
    shape = (3 * side, LANES)
    out = places(shape, 1)
    along = tap((places(shape, 0) - side - out + RIM).astype(F32))
    along = jnp.where(out < reach, along, 0.0)
    blank = jnp.zeros((side, LANES), F32)
    fa = jnp.concatenate(
        [
            jnp.concatenate(
                [along[h * side : (h + 1) * side] if u == t else blank for u in range(fold)], axis=1
            )
            for h in range(3)
            for t in range(fold)
        ],
        axis=0,
    )
    block = 3 * groups
    shape = (padded, fold * block)
    out, at = places(shape, 0), places(shape, 1)
    t = jnp.zeros(shape, jnp.int32)
    for k in range(1, fold):
        t = t + jnp.where(at >= k * block, 1, 0)
    source = (at - t * block) * fold + t - side
    fb = jnp.where(out < reach, tap((source - out + RIM).astype(F32)), 0.0)
    shape = (fold * groups, padded)
    row, out = places(shape, 0), places(shape, 1)
    t = jnp.zeros(shape, jnp.int32)
    for k in range(1, fold):
        t = t + jnp.where(row >= k * groups, 1, 0)
    source = (row - t * groups) * fold + t
    fc = jnp.where(out < reach, tap((out - RIM - source).astype(F32)), 0.0)
    shape = (LANES, LANES)
    out, at = places(shape, 0), places(shape, 1)
    back = tap((out - RIM - (at & (side - 1))).astype(F32))
    back = jnp.where(out < reach, back, 0.0)
    fd = jnp.concatenate(
        [jnp.where((at >= t * side) & (at < (t + 1) * side), back, 0.0) for t in range(fold)], axis=0
    )
    return fa, fb, fc, fd


def score_kernel(side, height, width, near, slope, loss):
    fa, fb, fc, fd = bands(side, -(-(side + 2 * RIM) // 8) * 8)
    rows3 = near[4].shape[0] // 2
    groups = rows3 // 3
    fold = LANES // side
    fields = [[], [], [], [], []]
    for v in range(3):
        strip = jnp.concatenate([near[3 * v + h] for h in range(3)], axis=1)
        image, target = strip[:rows3], strip[rows3:]
        for f, plane in enumerate([image, target, image * image, target * target, image * target]):
            fields[f].append(plane)
    stack = jnp.concatenate([fields[f][v] for f in range(5) for v in range(3)], axis=0)
    wide = jnp.dot(stack, fa, precision=HIGH, preferred_element_type=F32)
    columns = []
    for f in range(5):
        for ch in range(3):
            parts = []
            for t in range(fold):
                for v in range(3):
                    at = (f * 3 + v) * rows3 + ch * groups
                    parts.append(wide[at : at + groups, t * LANES : (t + 1) * LANES])
            columns.append(jnp.concatenate(parts, axis=0))
    tall = jnp.concatenate(columns, axis=1)
    maps = jnp.dot(fb, tall, precision=HIGH, preferred_element_type=F32)
    span = 3 * LANES
    score, pull = jax.vjp(similarity, *[maps[:, f * span : (f + 1) * span] for f in range(5)])
    parts = pull(jnp.full(score.shape, -STRUCT_WEIGHT, F32))
    row = lax.broadcasted_iota(jnp.int32, score.shape, 0)
    col = lax.broadcasted_iota(jnp.int32, (score.shape[0], LANES), 1)
    col = jnp.concatenate([col] * 3, axis=1)
    row_at = row - RIM + lax.axis_index("ty") * side
    col_at = col - RIM + lax.axis_index("tx") * side
    reach = side + 2 * RIM
    inside = (
        (row_at >= 0) & (row_at < height) & (col_at >= 0) & (col_at < width)
        & (row < reach) & (col < reach)
    )
    own = (row >= RIM) & (row < RIM + side) & (col >= RIM) & (col < RIM + side)
    coeffs = jnp.concatenate(
        [jnp.where(inside, parts[f], 0.0) for f in (0, 2, 4)], axis=1
    )
    low = jnp.dot(fc, coeffs, precision=HIGH, preferred_element_type=F32)
    rows = []
    for n in range(9):
        rows.append(
            jnp.concatenate(
                [
                    low[t * groups : (t + 1) * groups, n * LANES : (n + 1) * LANES]
                    for t in range(fold)
                ],
                axis=1,
            )
        )
    smooth = jnp.dot(
        jnp.concatenate(rows, axis=0), fd, precision=HIGH, preferred_element_type=F32
    )
    image, target = near[4][:rows3, :], near[4][rows3:, :]
    gap = image - target
    robust = jnp.sqrt(gap * gap + ROBUST_TERM)
    slope[...] = (
        smooth[:rows3]
        + 2.0 * image * smooth[rows3 : 2 * rows3]
        + target * smooth[2 * rows3 :]
        + (1.0 - STRUCT_WEIGHT) * gap / robust
    )
    total = (1.0 - STRUCT_WEIGHT) * jnp.sum(robust) + STRUCT_WEIGHT * jnp.sum(
        jnp.where(own, 1.0 - score, 0.0)
    )
    loss[...] = jnp.full(loss.shape, total, F32)


def score_entry(side, height, width, *refs):
    above, left, own, right, below = refs[:5]
    rows = own.shape[0]
    near = [above[h * rows : (h + 1) * rows, :] for h in range(3)]
    near += [left[...], own[...], right[...]]
    near += [below[h * rows : (h + 1) * rows, :] for h in range(3)]
    score_kernel(side, height, width, near, *refs[5:])


def backward_kernel(
    side, table, checks, prefix, behind, slope, reduce, stage,
    rhs, wide, grows, buf_a, buf_b, behinds, sums_a, sums_b, moments,
):
    lmax = stage.shape[0]
    per = lmax // SEGS
    pixels = prefix.shape[1]
    groups = pixels // LANES
    chunks = lmax * LANES // CHUNK
    wide[...] = jnp.zeros_like(wide)
    for ch in range(3):
        for j in range(groups):
            lanes = pl.ds(j * LANES, LANES)
            wide[pl.ds(6 + ch, 1), lanes] = slope[pl.ds(ch * groups + j, 1), :]
    for ch in range(3):
        row = wide[pl.ds(6 + ch, 1), :]
        hi = row.astype(BF16).astype(F32)
        grows[ch] = jnp.broadcast_to(row, (SEGS, pixels))
        wide[pl.ds(6 + ch, 1), :] = hi
        wide[pl.ds(22 + ch, 1), :] = hi
        wide[pl.ds(38 + ch, 1), :] = row - hi
    rhs[:, :pixels] = monomials(side)
    rhs[:, pixels:] = wide[...].astype(BF16)

    def product(n, buf, p):
        rows = pl.ds(pl.multiple_of(n * CHUNK, CHUNK), CHUNK)
        cols = slice(p * COLS, (p + 1) * COLS)
        buf[:, cols] = jnp.dot(table[rows, :], rhs[:, cols], preferred_element_type=F32)

    def reduced(n, sums, low):
        rows = pl.ds(pl.multiple_of(n * CHUNK, CHUNK), CHUNK)
        part = sums[...].astype(BF16)
        if low:
            part = (sums[...] - part.astype(F32)).astype(BF16)
        value = jnp.dot(part, reduce[...], preferred_element_type=F32)
        moments[rows, :] = moments[rows, :] + value if low else value

    lane = lax.broadcasted_iota(jnp.int32, (SEGS, LANES), 1)
    front = lane < LANES // 2
    even = (lane & (LANES // 4)) == 0

    def folded(a, b):
        return jnp.where(front, a, b) + pltpu.roll(jnp.where(front, b, a), LANES // 2, 1)

    def packed(a, b, c, d):
        ab, cd = folded(a, b), folded(c, d)
        ab = ab + pltpu.roll(ab, LANES - LANES // 4, 1)
        cd = cd + pltpu.roll(cd, LANES // 4, 1)
        return jnp.where(even, ab, cd)

    def block(n, b, buf, sums):
        first = b * SPAN * SEGS
        rows = [pl.ds(first + i * SEGS, SEGS) for i in range(SPAN)]
        totals = [[None] * 6 for _ in range(SPAN)]

        def add(i, f, value):
            totals[i][f] = value if totals[i][f] is None else totals[i][f] + value

        for q in reversed(range(groups // 2)):
            lanes = slice(q * 2 * LANES, (q + 1) * 2 * LANES)
            light = checks[n * (STEPS // SPAN) + b, :, lanes] * prefix[:, lanes]
            tints = [grows[ch, :, lanes] for ch in range(3)]
            alphas, weights = [], []
            for i in range(SPAN):
                alphas.append(jnp.exp2(buf[rows[i], lanes]))
                weights.append(light * alphas[i])
                light = light - weights[i]
            back = behinds[:, lanes]
            for i in reversed(range(SPAN)):
                gap = buf[rows[i], pixels + q * 2 * LANES : pixels + (q + 1) * 2 * LANES] - back
                back = back + alphas[i] * gap
                pull = weights[i] * gap
                add(i, 0, pull[:, LANES:])
                add(i, 1, totals[i][0])
                add(i, 2, totals[i][1])
                add(i, 0, pull[:, :LANES])
                if q > 0:
                    add(i, 1, totals[i][0])
                    add(i, 2, totals[i][1])
                for ch in range(3):
                    tint = weights[i] * tints[ch]
                    add(i, 3 + ch, tint[:, LANES:] + tint[:, :LANES])
            behinds[:, lanes] = back
        for i in range(SPAN):
            zero, one, two, red, green, blue = totals[i]
            sums[rows[i], 0:LANES] = zero
            sums[rows[i], LANES : 2 * LANES] = one
            sums[rows[i], 2 * LANES : 3 * LANES] = packed(red, green, blue, two)

    behinds[...] = behind[0] * grows[0] + behind[1] * grows[1] + behind[2] * grows[2]
    pieces = 2 * pixels // COLS
    for p in range(pieces):
        product(chunks - 1, buf_a, p)
    turn = chunks // per
    share = SEGS // turn

    def collect(m, seg):
        moved = moments[pl.ds(m * (SEGS * LANES) + seg, LANES, stride=SEGS), :].T
        stage[seg * per + m] = moved[:16]

    def half(n, ahead, buf, other, sums, last, seg):
        m = (n // turn + 1) % per
        spans = STEPS // SPAN
        for at in range(spans):
            for p in range(at * pieces // spans, (at + 1) * pieces // spans):
                product(ahead, other, p)
            if at == 1 or at == 3:
                reduced(n + 1, last, at == 3)
            block(n, spans - 1 - at, buf, sums)
        for q in range(share):
            collect(m, seg * share + q)

    def pair(h, _):
        n = chunks - 1 - 2 * h
        half(n, n - 1, buf_a, buf_b, sums_a, sums_b, n % turn)
        half(n - 1, jnp.maximum(n - 2, 0), buf_b, buf_a, sums_b, sums_a, n % turn - 1)
        return 0

    lax.fori_loop(0, chunks // 2, pair, 0)
    reduced(0, sums_b, False)
    reduced(0, sums_b, True)
    for seg in range(SEGS):
        collect(0, seg)


def deliver_kernel(slot, stage, *refs):
    reply = refs[-1]
    column = refs[0][...]
    for share in refs[1:-1]:
        column = column + share[...]
    for o in range(reply.shape[0]):
        reply[o, pl.ds(reply.shape[1] - 1, 1), :] = column[:1]
    for k in range(slot.shape[0]):
        s = slot[k]
        o = s // CAP
        c = s - o * CAP
        reply[o, pl.ds(pl.multiple_of(c * 8, 8), 8), :] = stage[k, :8, :]
        reply[o, pl.ds(CAP * 8 + c, 1), :] = stage[k, 8:9, :]


def gather_kernel(
    across, side, height, width, asked, got, gaussians, grads, loss, sums, zeros, pieces, wanted, sem
):
    owned = gaussians.shape[1]
    parts = owned // 8
    shares = got[:, got.shape[1] - 1, :]
    loss[0] = jnp.sum(shares[:, :1]) * (1.0 / (3.0 * height * width))
    zeros[...] = jnp.zeros_like(zeros)
    sums[...] = jnp.zeros_like(sums)
    for g in range(parts + 1):
        wanted[g] = 0
    for s in range(across * CAP):
        c, t = divmod(s, across)
        index = asked[t, 0, c]
        index = jnp.where(index >= 0, index, owned)
        wanted[index // 8] = 1
        row = pl.ds(index, 1)
        for f in range(9):
            at = c * 8 + f if f < 8 else CAP * 8 + c
            sums[f, row, :] = got[t, at : at + 1, :]
        sums[9, row, :] = jnp.full((1, LANES), t + 1.0, F32)

    def target(g):
        return grads.at[:, pl.ds(pl.multiple_of(g * 8, 8), 8), :]

    def blank(g, _):
        @pl.when(wanted[g] == 0)
        def _():
            pltpu.make_async_copy(zeros, target(g), sem.at[g]).start()

        return 0

    lax.fori_loop(0, parts, blank, 0)
    row_at = lax.axis_index("ty").astype(F32)
    shift_y = (0.5 * height - 0.5 * side - 0.5) - side * row_at

    def solve(g):
        rows = pl.ds(pl.multiple_of(g * 8, 8), 8)
        field = [gaussians[f, rows, :] for f in range(11)]
        tile = sums[9, rows, :]
        live = tile > 0.0
        shift_x = (0.5 * width - 0.5 * side - 0.5) - side * (tile - 1.0)

        def put(f, value):
            pieces[g, f] = jnp.where(live, value, 0.0)

        def shaped(x, y, z, log_scale, quat):
            xx, xy, yy, pos_u, pos_v = conic(x, y, z, log_scale, quat)
            return expanded(xx, xy, yy, pos_u + shift_x, pos_v + shift_y, jnp.zeros_like(x))

        _, pull = jax.vjp(shaped, *field[:3], field[3:6], field[6:10])
        moments = [LN2 * sums[f, rows, :] for f in range(6)]
        gx, gy, gz, gscale, gquat = pull(tuple(moments))
        basis, pull_basis = jax.vjp(directions, *field[:3])
        tints = [sums[6 + ch, rows, :] for ch in range(3)]
        tilts = []
        for m in range(16):
            tilt = None
            for ch in range(3):
                term = tints[ch] * gaussians[11 + 3 * m + ch, rows, :]
                tilt = term if tilt is None else tilt + term
                put(11 + 3 * m + ch, tints[ch] * basis[m])
            tilts.append(tilt)
        dx, dy, dz = pull_basis(tilts)
        put(0, gx + dx)
        put(1, gy + dy)
        put(2, gz + dz)
        for f in range(3):
            put(3 + f, gscale[f])
        for f in range(4):
            put(6 + f, gquat[f])
        put(10, moments[5] * (LOG2E / (1.0 + jnp.exp(field[10]))))
        pltpu.make_async_copy(pieces.at[g], target(g), sem.at[g]).start()

    def part(g, _):
        @pl.when(wanted[g] > 0)
        def _():
            solve(g)

        return 0

    lax.fori_loop(0, parts, part, 0)

    def finish(g, _):
        pltpu.make_async_copy(zeros, target(g), sem.at[g]).wait()
        return 0

    lax.fori_loop(0, parts, finish, 0)


def moment_columns(side):
    lane = np.arange(LANES)
    x = lane % side - side // 2
    t = lane // side - side // 2
    step = LANES // side
    one = np.ones_like(x)
    out = np.zeros((3 * LANES, LANES))
    out[:LANES, :6] = np.stack([x * x, x * t, t * t, x, t, one], axis=1)
    out[LANES : 2 * LANES, 1] = step * x
    out[LANES : 2 * LANES, 2] = 2 * step * t - step * step
    out[LANES : 2 * LANES, 4] = step
    quarter = LANES // 4
    for n, (column, weight) in enumerate(((6, 1), (8, 1), (7, 1), (2, 2 * step * step))):
        at = 2 * LANES + n * quarter
        out[at : at + quarter, column] = weight
    return out.astype(ml_dtypes.bfloat16)


def shifted(x, axis):
    size = lax.axis_size(axis)
    up = [(i, i + 1) for i in range(size - 1)]
    return lax.ppermute(x, axis, up), lax.ppermute(x, axis, [(j, i) for i, j in up])


def per_device(gaussians, tile_lists, tile_counts, depth_order, target):
    owned, fields, block = gaussians.shape
    lmax = tile_lists.shape[2]
    side = target.shape[1]
    pixels = side * side
    groups = pixels // LANES
    across = lax.axis_size("tx")
    down = lax.axis_size("ty")
    height = side * lax.axis_size("ty")
    width = side * across
    slots = across * CAP
    depth = -(-(CAP * 9 + 1) // 8) * 8
    f32 = functools.partial(jax.ShapeDtypeStruct, dtype=F32)
    i32 = functools.partial(jax.ShapeDtypeStruct, dtype=jnp.int32)
    reduce = jnp.asarray(moment_columns(side))

    fieldwise = jnp.transpose(gaussians, (1, 0, 2))
    request, slot = pl.pallas_call(
        functools.partial(request_kernel, owned, across),
        out_shape=(i32((across, 1, LANES)), i32((lmax,))),
        in_specs=[SMEM] * 3,
        out_specs=(SMEM, SMEM),
        scratch_shapes=[pltpu.SMEM((across,), jnp.int32)],
        name="request",
    )(tile_lists, tile_counts, depth_order)
    asked = lax.all_to_all(request, "tx", split_axis=0, concat_axis=0, tiled=True)
    projected = pl.pallas_call(
        functools.partial(project_kernel, 16),
        out_shape=f32((9, owned, block)),
        in_specs=[VMEM],
        out_specs=VMEM,
        compiler_params=PARAMS,
        name="project",
    )(fieldwise)
    send = pl.pallas_call(
        functools.partial(serve_kernel, across, side, float(height), float(width)),
        out_shape=f32((across, depth, block)),
        in_specs=[SMEM, VMEM],
        out_specs=VMEM,
        scratch_shapes=[pltpu.VMEM((9, slots, block), F32)],
        compiler_params=PARAMS,
        name="serve",
    )(asked, projected)
    recv = lax.all_to_all(send, "tx", split_axis=0, concat_axis=0, tiled=True)
    chunks = lmax * block // CHUNK
    wide = pixels + 3 * LANES
    table, checks, prefix, behind, dense = pl.pallas_call(
        functools.partial(forward_kernel, side),
        out_shape=(
            jax.ShapeDtypeStruct((lmax * block, LANES), BF16),
            f32((chunks * (STEPS // SPAN), SEGS, pixels)),
            f32((SEGS, pixels)),
            f32((3, SEGS, pixels)),
            f32((6 * groups, LANES)),
        ),
        in_specs=[SMEM, SMEM, VMEM, VMEM],
        out_specs=(VMEM,) * 5,
        scratch_shapes=[
            pltpu.VMEM((LANES, wide), BF16),
            pltpu.VMEM((lmax * block, LANES), F32),
            pltpu.VMEM((CHUNK, wide), F32),
            pltpu.VMEM((CHUNK, wide), F32),
            pltpu.VMEM((4, SEGS, pixels), F32),
        ],
        compiler_params=PARAMS,
        name="forward",
    )(slot, tile_counts, recv, target.reshape(3 * groups, LANES))
    left, right = shifted(dense, "tx")
    above, below = shifted(jnp.concatenate([left, dense, right], axis=0), "ty")
    slope, part = pl.pallas_call(
        functools.partial(score_entry, side, height, width),
        out_shape=(f32((3 * groups, LANES)), f32((8, LANES))),
        in_specs=[VMEM] * 5,
        out_specs=(VMEM, VMEM),
        compiler_params=PARAMS,
        name="score",
    )(above, left, dense, right, below)
    shares = [
        lax.ppermute(part, "ty", [(i, (i + k) % down) for i in range(down)]) for k in range(1, down)
    ]
    stage = pl.pallas_call(
        functools.partial(backward_kernel, side),
        out_shape=f32((lmax, 16, LANES)),
        in_specs=[VMEM] * 6,
        out_specs=VMEM,
        scratch_shapes=[
            pltpu.VMEM((LANES, 2 * pixels), BF16),
            pltpu.VMEM((LANES, pixels), F32),
            pltpu.VMEM((3, SEGS, pixels), F32),
            pltpu.VMEM((CHUNK, 2 * pixels), F32),
            pltpu.VMEM((CHUNK, 2 * pixels), F32),
            pltpu.VMEM((SEGS, pixels), F32),
            pltpu.VMEM((CHUNK, 3 * LANES), F32),
            pltpu.VMEM((CHUNK, 3 * LANES), F32),
            pltpu.VMEM((lmax * block + CHUNK, LANES), F32),
        ],
        compiler_params=PARAMS,
        name="backward",
    )(table, checks, prefix, behind, slope, reduce)
    reply = pl.pallas_call(
        deliver_kernel,
        out_shape=f32((across, depth, block)),
        in_specs=[SMEM] + [VMEM] * (1 + down),
        out_specs=VMEM,
        compiler_params=PARAMS,
        name="deliver",
    )(slot, stage, part, *shares)
    got = lax.all_to_all(reply, "tx", split_axis=0, concat_axis=0, tiled=True)
    grads, loss = pl.pallas_call(
        functools.partial(gather_kernel, across, side, float(height), float(width)),
        out_shape=(f32((fields, owned, block)), f32((1,))),
        in_specs=[SMEM, VMEM, VMEM],
        out_specs=(ANY, SMEM),
        scratch_shapes=[
            pltpu.VMEM((10, owned + 8, block), F32),
            pltpu.VMEM((fields, 8, block), F32),
            pltpu.VMEM((owned // 8, fields, 8, block), F32),
            pltpu.SMEM((owned // 8 + 1,), jnp.int32),
            pltpu.SemaphoreType.DMA((owned // 8,)),
        ],
        compiler_params=PARAMS,
        name="gather",
    )(asked, got, fieldwise)
    return (jnp.transpose(grads, (1, 0, 2)), loss[0])


def solution(mesh):
    return jax.shard_map(
        per_device,
        mesh=mesh,
        in_specs=(
            P(("ty", "tx"), None, None),
            P("ty", "tx", None),
            P("ty", "tx"),
            P(),
            P(None, "ty", "tx"),
        ),
        out_specs=(P(("ty", "tx"), None, None), P()),
        check_vma=False,
    )
```

profile of v0, /device:TPU:0, one launch (start us, length us, event | category | flops | bytes accessed | tf_op | source)
XLA Modules:
  0.0 83.5 jit_solution(9715001137681397926)
XLA Ops:
  1.3 1.8 %request.1 = (s32[8,1,128]{2,1,0:T(1,128)}, s32[24]{0:T(128)}) custom-call(s32[1,1,24]{2,1,0:T(1,128)} %lists.1, s32[1,1]{1,0:T(1,128)S(6)} %copy.10.count, s32[3072]{0:T(1024)} %order.1), custom_call_target="tpu_custom_call" | custom-call | tf_op jit(solution)/shard_map/request/pallas_call | solution.py:753
  3.1 7.3 %all-to-all-start = ((s32[8,1,128]{2,1,0:T(1,128)}), s32[8,1,128]{2,1,0:T(1,128)S(1)}, u32[]{:S(2)}, u32[]{:S(2)}) async-start(s32[8,1,128]{2,1,0:T(1,128)} %get-tuple-element.13), calls=%async_computation | async-start | bytes 8192 | tf_op jit(solution)/shard_map/all_to_all | solution.py:761
  10.4 1.8 %copy-done = f32[96,59,128]{2,0,1:T(8,128)S(1)} copy-done((f32[96,59,128]{2,0,1:T(8,128)S(1)}, f32[96,59,128]{2,0,1:T(8,128)}, u32[]{:S(2)}) %copy-start) | copy-done | bytes 2899992
  12.2 0.6 project.1.projected
  12.8 3.9 %all-to-all-done.asked = s32[8,1,128]{2,1,0:T(1,128)S(1)} async-done(((s32[8,1,128]{2,1,0:T(1,128)}), s32[8,1,128]{2,1,0:T(1,128)S(1)}, u32[]{:S(2)}, u32[]{:S(2)}) %all-to-all-start) | async-done | bytes 4128 | tf_op jit(solution)/shard_map/all_to_all | solution.py:761
  16.8 1.4 %serve.1 = f32[8,32,128]{2,1,0:T(8,128)} custom-call(s32[8,1,128]{2,1,0:T(1,128)S(1)} %all-to-all-done.asked, f32[9,96,128]{2,1,0:T(8,128)S(1)} %project.1.projected), custom_call_target="tpu_custom_call" | custom-call | tf_op jit(solution)/shard_map/serve/pallas_call | solution.py:770
  18.2 3.6 %all-to-all-start.1 = ((f32[8,32,128]{2,1,0:T(8,128)}), f32[8,32,128]{2,1,0:T(8,128)S(1)}, u32[]{:S(2)}, u32[]{:S(2)}) async-start(f32[8,32,128]{2,1,0:T(8,128)} %serve.1), calls=%async_computation.1 | async-start | bytes 262144 | tf_op jit(solution)/shard_map/all_to_all | solution.py:779
  21.9 7.2 %all-to-all-done.1.recv = f32[8,32,128]{2,1,0:T(8,128)S(1)} async-done(((f32[8,32,128]{2,1,0:T(8,128)}), f32[8,32,128]{2,1,0:T(8,128)S(1)}, u32[]{:S(2)}, u32[]{:S(2)}) %all-to-all-start.1) | async-done | bytes 131104 | tf_op jit(solution)/shard_map/all_to_all | solution.py:779
  29.1 7.4 %forward.1 = (bf16[3072,128]{1,0:T(8,128)(2,1)S(1)}, f32[96,8,1024]{2,1,0:T(8,128)S(1)}, f32[8,1024]{1,0:T(8,128)S(1)}, f32[3,8,1024]{2,1,0:T(8,128)S(1)}, f32[48,128]{1,0:T(8,128)S(1)}) custom-call(s32[24]{0:T(128)S(1)} %copy-done.3, s32[1,1]{1,0:T(1,128)S(6)} %copy.10.count, f32[8,32,128]{2,1,0:T(8,128)S(1)} %all-to-all-done.1.recv, ...), custom_call_target="tpu_custom_call" | custom-call | tf_op jit(solution)/shard_map/forward/pallas_call | solution.py:782
  36.5 2.1 %collective-permute-start = (f32[48,128]{1,0:T(8,128)S(1)}, f32[48,128]{1,0:T(8,128)S(1)}, u32[]{:S(2)}, u32[]{:S(2)}) collective-permute-start(f32[48,128]{1,0:T(8,128)S(1)} %get-tuple-element.19.refs_2_), channel_id=1, source_target_pairs={{0,1},{1,2},{2,3},{3,4},{4,5},{5,6},{6,7},{8,9},{9,10},{10,11},{11... | collective-permute-start | bytes 73736 | tf_op jit(solution)/shard_map/ppermute | solution.py:733
  38.7 1.3 %collective-permute-start.1 = (f32[48,128]{1,0:T(8,128)S(1)}, f32[48,128]{1,0:T(8,128)S(1)}, u32[]{:S(2)}, u32[]{:S(2)}) collective-permute-start(f32[48,128]{1,0:T(8,128)S(1)} %get-tuple-element.19.refs_2_), channel_id=1, source_target_pairs={{1,0},{2,1},{3,2},{4,3},{5,4},{6,5},{7,6},{9,8},{10,9},{11,10},{12... | collective-permute-start | bytes 73736 | tf_op jit(solution)/shard_map/ppermute | solution.py:733
  40.0 0.3 collective-permute-done.refs_1_
  40.3 4.1 %collective-permute-done.1.refs_3_ = f32[48,128]{1,0:T(8,128)S(1)} collective-permute-done((f32[48,128]{1,0:T(8,128)S(1)}, f32[48,128]{1,0:T(8,128)S(1)}, u32[]{:S(2)}, u32[]{:S(2)}) %collective-permute-start.1) | collective-permute-done | bytes 24608 | tf_op jit(solution)/shard_map/ppermute | solution.py:733
  44.4 1.3 %collective-permute-start.3 = (f32[144,128]{1,0:T(8,128)S(1)}, f32[144,128]{1,0:T(8,128)S(1)}, u32[]{:S(2)}, u32[]{:S(2)}) collective-permute-start(f32[144,128]{1,0:T(8,128)S(1)} %constant_dynamic-update-slice_fusion), channel_id=1, source_target_pairs={{8,0},{16,8},{24,16},{9,1},{17,9},{25,17},{10,2},{18,10},{26,18},{... | collective-permute-start | bytes 221192 | tf_op jit(solution)/shard_map/ppermute | solution.py:733
  45.7 3.0 %collective-permute-start.2 = (f32[144,128]{1,0:T(8,128)S(1)}, f32[144,128]{1,0:T(8,128)S(1)}, u32[]{:S(2)}, u32[]{:S(2)}) collective-permute-start(f32[144,128]{1,0:T(8,128)S(1)} %constant_dynamic-update-slice_fusion), channel_id=1, source_target_pairs={{0,8},{8,16},{16,24},{1,9},{9,17},{17,25},{2,10},{10,18},{18,26},{... | collective-permute-start | bytes 221192 | tf_op jit(solution)/shard_map/ppermute | solution.py:733
  48.7 0.9 %collective-permute-done.2.refs_0_ = f32[144,128]{1,0:T(8,128)S(1)} collective-permute-done((f32[144,128]{1,0:T(8,128)S(1)}, f32[144,128]{1,0:T(8,128)S(1)}, u32[]{:S(2)}, u32[]{:S(2)}) %collective-permute-start.2) | collective-permute-done | bytes 73760 | tf_op jit(solution)/shard_map/ppermute | solution.py:733
  49.6 2.6 %score.1 = (f32[24,128]{1,0:T(8,128)S(1)}, f32[8,128]{1,0:T(8,128)S(1)}) custom-call(f32[144,128]{1,0:T(8,128)S(1)} %collective-permute-done.2.refs_0_, f32[48,128]{1,0:T(8,128)S(1)} %collective-permute-done.refs_1_, f32[48,128]{1,0:T(8,128)S(1)} %get-tuple-element.19.refs_2_, f32[48,128]{1,0:T(8,128)S(1)} %collective-permute-done.1.refs_3_, ...), custom_call_target="tpu_custom_call" | custom-call | tf_op jit(solution)/shard_map/score/pallas_call | solution.py:805
  52.3 1.5 %collective-permute-start.6 = (f32[8,128]{1,0:T(8,128)S(1)}, f32[8,128]{1,0:T(8,128)S(1)}, u32[]{:S(2)}, u32[]{:S(2)}) collective-permute-start(f32[8,128]{1,0:T(8,128)S(1)} %get-tuple-element.21.refs_0_), channel_id=1, source_target_pairs={{0,24},{8,0},{16,8},{24,16},{1,25},{9,1},{17,9},{25,17},{2,26},{10... | collective-permute-start | bytes 12296 | tf_op jit(solution)/shard_map/ppermute | solution.py:814
  53.8 2.5 %collective-permute-start.5 = (f32[8,128]{1,0:T(8,128)S(1)}, f32[8,128]{1,0:T(8,128)S(1)}, u32[]{:S(2)}, u32[]{:S(2)}) collective-permute-start(f32[8,128]{1,0:T(8,128)S(1)} %get-tuple-element.21.refs_0_), channel_id=1, source_target_pairs={{0,16},{8,24},{16,0},{24,8},{1,17},{9,25},{17,1},{25,9},{2,18},{10... | collective-permute-start | bytes 12296 | tf_op jit(solution)/shard_map/ppermute | solution.py:814
  56.2 0.2 collective-permute-start.4
  56.4 12.2 %backward.1.stage = f32[24,16,128]{2,1,0:T(8,128)S(1)} custom-call(bf16[3072,128]{1,0:T(8,128)(2,1)S(1)} %get-tuple-element.15.table, f32[96,8,1024]{2,1,0:T(8,128)S(1)} %get-tuple-element.16.checks, f32[8,1024]{1,0:T(8,128)S(1)} %get-tuple-element.17.prefix, f32[3,8,1024]{2,1,0:T(8,128)S(1)} %get-tuple-element.18.behind, ...), custom_call_target="tpu_custom_call" | custom-call | tf_op jit(solution)/shard_map/backward/pallas_call | solution.py:816
  68.6 0.7 deliver.1
  69.4 11.1 %all_to_all.15.got = f32[8,32,128]{2,1,0:T(8,128)S(1)} all-to-all(f32[8,32,128]{2,1,0:T(8,128)S(1)} %deliver.1), channel_id=1, replica_groups=mesh['ty'=4,'tx'=8] {'tx'}, dimensions={0} | all-to-all | bytes 262144 | tf_op jit(solution)/shard_map/all_to_all | solution.py:843
  80.5 3.0 %gather.1 = (f32[59,96,128]{2,1,0:T(8,128)}, f32[1]{0:T(128)}) custom-call(s32[8,1,128]{2,1,0:T(1,128)S(1)} %all-to-all-done.asked, f32[8,32,128]{2,1,0:T(8,128)S(1)} %all_to_all.15.got, f32[59,96,128]{2,1,0:T(8,128)S(1)} %bitcast.4), custom_call_target="tpu_custom_call" | custom-call | tf_op jit(solution)/shard_map/gather/pallas_call | solution.py:844
  (17 shorter events, 0.1 us)
Async XLA Ops:
  3.1 26.0 %copy-start.3 = (s32[24]{0:T(128)S(1)}, s32[24]{0:T(128)}, u32[]{:S(2)}) copy-start(s32[24]{0:T(128)} %get-tuple-element.14.slot) | copy-start | bytes 292
  3.1 13.7 %all-to-all-start = ((s32[8,1,128]{2,1,0:T(1,128)}), s32[8,1,128]{2,1,0:T(1,128)S(1)}, u32[]{:S(2)}, u32[]{:S(2)}) async-start(s32[8,1,128]{2,1,0:T(1,128)} %get-tuple-element.13), calls=%async_computation | async-start | bytes 8192 | tf_op jit(solution)/shard_map/all_to_all | solution.py:761
  10.4 1.8 %copy-start = (f32[96,59,128]{2,0,1:T(8,128)S(1)}, f32[96,59,128]{2,0,1:T(8,128)}, u32[]{:S(2)}) copy-start(f32[96,59,128]{2,0,1:T(8,128)} %param.6) | copy-start | bytes 8699908
  12.2 9.6 %copy-start.4 = (f32[3,32,32]{2,1,0:T(8,128)S(1)}, f32[3,32,32]{2,1,0:T(8,128)}, u32[]{:S(2)}) copy-start(f32[3,32,32]{2,1,0:T(8,128)} %param.10) | copy-start | bytes 36868
  12.2 44.2 %copy-start.2 = (bf16[384,128]{1,0:T(8,128)(2,1)S(1)}, bf16[384,128]{1,0:T(8,128)(2,1)}, u32[]{:S(2)}) copy-start(bf16[384,128]{1,0:T(8,128)(2,1)} %constant.2.clone.reduce) | copy-start | bytes 294916
  18.2 62.3 %copy-start.1 = (f32[96,59,128]{2,0,1:T(8,128)S(1)}, f32[96,59,128]{2,0,1:T(8,128)}, u32[]{:S(2)}) copy-start(f32[96,59,128]{2,0,1:T(8,128)} %param.6) | copy-start | bytes 8699908
  18.2 10.9 %all-to-all-start.1 = ((f32[8,32,128]{2,1,0:T(8,128)}), f32[8,32,128]{2,1,0:T(8,128)S(1)}, u32[]{:S(2)}, u32[]{:S(2)}) async-start(f32[8,32,128]{2,1,0:T(8,128)} %serve.1), calls=%async_computation.1 | async-start | bytes 262144 | tf_op jit(solution)/shard_map/all_to_all | solution.py:779
  36.5 3.7 %collective-permute-start = (f32[48,128]{1,0:T(8,128)S(1)}, f32[48,128]{1,0:T(8,128)S(1)}, u32[]{:S(2)}, u32[]{:S(2)}) collective-permute-start(f32[48,128]{1,0:T(8,128)S(1)} %get-tuple-element.19.refs_2_), channel_id=1, source_target_pairs={{0,1},{1,2},{2,3},{3,4},{4,5},{5,6},{6,7},{8,9},{9,10},{10,11},{11... | collective-permute-start | bytes 73736 | tf_op jit(solution)/shard_map/ppermute | solution.py:733
  38.7 5.7 %collective-permute-start.1 = (f32[48,128]{1,0:T(8,128)S(1)}, f32[48,128]{1,0:T(8,128)S(1)}, u32[]{:S(2)}, u32[]{:S(2)}) collective-permute-start(f32[48,128]{1,0:T(8,128)S(1)} %get-tuple-element.19.refs_2_), channel_id=1, source_target_pairs={{1,0},{2,1},{3,2},{4,3},{5,4},{6,5},{7,6},{9,8},{10,9},{11,10},{12... | collective-permute-start | bytes 73736 | tf_op jit(solution)/shard_map/ppermute | solution.py:733
  44.4 4.3 %collective-permute-start.3 = (f32[144,128]{1,0:T(8,128)S(1)}, f32[144,128]{1,0:T(8,128)S(1)}, u32[]{:S(2)}, u32[]{:S(2)}) collective-permute-start(f32[144,128]{1,0:T(8,128)S(1)} %constant_dynamic-update-slice_fusion), channel_id=1, source_target_pairs={{8,0},{16,8},{24,16},{9,1},{17,9},{25,17},{10,2},{18,10},{26,18},{... | collective-permute-start | bytes 221192 | tf_op jit(solution)/shard_map/ppermute | solution.py:733
  45.7 3.9 %collective-permute-start.2 = (f32[144,128]{1,0:T(8,128)S(1)}, f32[144,128]{1,0:T(8,128)S(1)}, u32[]{:S(2)}, u32[]{:S(2)}) collective-permute-start(f32[144,128]{1,0:T(8,128)S(1)} %constant_dynamic-update-slice_fusion), channel_id=1, source_target_pairs={{0,8},{8,16},{16,24},{1,9},{9,17},{17,25},{2,10},{10,18},{18,26},{... | collective-permute-start | bytes 221192 | tf_op jit(solution)/shard_map/ppermute | solution.py:733
  52.3 16.4 %collective-permute-start.6 = (f32[8,128]{1,0:T(8,128)S(1)}, f32[8,128]{1,0:T(8,128)S(1)}, u32[]{:S(2)}, u32[]{:S(2)}) collective-permute-start(f32[8,128]{1,0:T(8,128)S(1)} %get-tuple-element.21.refs_0_), channel_id=1, source_target_pairs={{0,24},{8,0},{16,8},{24,16},{1,25},{9,1},{17,9},{25,17},{2,26},{10... | collective-permute-start | bytes 12296 | tf_op jit(solution)/shard_map/ppermute | solution.py:814
  53.8 14.9 %collective-permute-start.5 = (f32[8,128]{1,0:T(8,128)S(1)}, f32[8,128]{1,0:T(8,128)S(1)}, u32[]{:S(2)}, u32[]{:S(2)}) collective-permute-start(f32[8,128]{1,0:T(8,128)S(1)} %get-tuple-element.21.refs_0_), channel_id=1, source_target_pairs={{0,16},{8,24},{16,0},{24,8},{1,17},{9,25},{17,1},{25,9},{2,18},{10... | collective-permute-start | bytes 12296 | tf_op jit(solution)/shard_map/ppermute | solution.py:814
  56.2 12.4 %collective-permute-start.4 = (f32[8,128]{1,0:T(8,128)S(1)}, f32[8,128]{1,0:T(8,128)S(1)}, u32[]{:S(2)}, u32[]{:S(2)}) collective-permute-start(f32[8,128]{1,0:T(8,128)S(1)} %get-tuple-element.21.refs_0_), channel_id=1, source_target_pairs={{0,8},{8,16},{16,24},{24,0},{1,9},{9,17},{17,25},{25,1},{2,10},{10... | collective-permute-start | bytes 12296 | tf_op jit(solution)/shard_map/ppermute | solution.py:814
where the time goes:
time: 84 us; the launch traced here: 83.5 us
  Pallas kernels  29.8 us (35%)
  starting transfers between devices  22.8 us (27%)
  waiting for transfers between devices  16.5 us (20%)
  blocking collectives  11.1 us (13%)
  local copies, waits for them, and re-layouts  1.92 us (2%)
  between operations  1.4 us (2%)
    pallas_call x1, Pallas kernels, per_device(): pl.pallas_call(functools.partial(backward_kernel, side), out_shape=f32((l...  12.2 us
    all_to_all x1, blocking collectives, per_device(): got = lax.all_to_all(reply, 'tx', split_axis=0, concat_axis=0, tiled=True)  11.1 us
    pallas_call x1, Pallas kernels, per_device(): pl.pallas_call(functools.partial(forward_kernel, side), out_shape=(jax.Sh...  7.4 us
    all_to_all x1, starting transfers between devices, per_device(): lax.all_to_all(request, 'tx', split_axis=0, concat_axis=0, tiled=True)  7.28 us
    all_to_all x1, waiting for transfers between devices, per_device(): recv = lax.all_to_all(send, 'tx', split_axis=0, concat_axis=0, tiled=True)  7.19 us
    ppermute x2, starting transfers between devices, shifted(): lax.ppermute(x, axis, up)  5.15 us
    ppermute x3, starting transfers between devices, per_device(): lax.ppermute(part, 'ty', [(i, (i + k) % down) for i in range(down)])  4.16 us
    ppermute x2, waiting for transfers between devices, shifted(): lax.ppermute(x, axis, [(j, i) for i, j in up])  4.13 us
  transfers between devices with their start and end apart: 9, of which 5 were waited for; matrix products, arithmetic and copies ran while one was open for 0% of the time, Pallas kernels for 15%

commit v1 on v0

--- a/solution.py
+++ b/solution.py
@@ -239,7 +239,7 @@
 
 
 def forward_kernel(
-    side, slot, count, recv, target, table, checks, prefix, behind, dense,
+    side, slot, count, recv, target, table, alphas, checks, prefix, behind, dense,
     planes, spread, buf_a, buf_b, ends,
 ):
     lmax = slot.shape[0]
@@ -288,7 +288,9 @@
         checks[n * (STEPS // SPAN) + b] = light
         for i in range(b * SPAN, (b + 1) * SPAN):
             rows = pl.ds(i * SEGS, SEGS)
-            weight = light * jnp.exp2(buf[rows, :pixels])
+            alpha = jnp.exp2(buf[rows, :pixels])
+            alphas[pl.ds(pl.multiple_of(n * CHUNK + i * SEGS, SEGS), SEGS), :] = alpha
+            weight = light * alpha
             light = light - weight
             red = red + weight * repeated(buf[rows, pixels : pixels + LANES], groups)
             green = green + weight * repeated(buf[rows, pixels + LANES : pixels + 2 * LANES], groups)
@@ -480,7 +482,7 @@
 
 
 def backward_kernel(
-    side, table, checks, prefix, behind, slope, reduce, stage,
+    table, alphas, checks, prefix, behind, slope, reduce, stage,
     rhs, wide, grows, buf_a, buf_b, behinds, sums_a, sums_b, moments,
 ):
     lmax = stage.shape[0]
@@ -500,8 +502,7 @@
         wide[pl.ds(6 + ch, 1), :] = hi
         wide[pl.ds(22 + ch, 1), :] = hi
         wide[pl.ds(38 + ch, 1), :] = row - hi
-    rhs[:, :pixels] = monomials(side)
-    rhs[:, pixels:] = wide[...].astype(BF16)
+    rhs[...] = wide[...].astype(BF16)
 
     def product(n, buf, p):
         rows = pl.ds(pl.multiple_of(n * CHUNK, CHUNK), CHUNK)
@@ -541,15 +542,16 @@
             lanes = slice(q * 2 * LANES, (q + 1) * 2 * LANES)
             light = checks[n * (STEPS // SPAN) + b, :, lanes] * prefix[:, lanes]
             tints = [grows[ch, :, lanes] for ch in range(3)]
-            alphas, weights = [], []
+            kept, weights = [], []
             for i in range(SPAN):
-                alphas.append(jnp.exp2(buf[rows[i], lanes]))
-                weights.append(light * alphas[i])
+                at = pl.multiple_of(n * CHUNK + first + i * SEGS, SEGS)
+                kept.append(alphas[pl.ds(at, SEGS), lanes])
+                weights.append(light * kept[i])
                 light = light - weights[i]
             back = behinds[:, lanes]
             for i in reversed(range(SPAN)):
-                gap = buf[rows[i], pixels + q * 2 * LANES : pixels + (q + 1) * 2 * LANES] - back
-                back = back + alphas[i] * gap
+                gap = buf[rows[i], lanes] - back
+                back = back + kept[i] * gap
                 pull = weights[i] * gap
                 add(i, 0, pull[:, LANES:])
                 add(i, 1, totals[i][0])
@@ -569,7 +571,7 @@
             sums[rows[i], 2 * LANES : 3 * LANES] = packed(red, green, blue, two)
 
     behinds[...] = behind[0] * grows[0] + behind[1] * grows[1] + behind[2] * grows[2]
-    pieces = 2 * pixels // COLS
+    pieces = pixels // COLS
     for p in range(pieces):
         product(chunks - 1, buf_a, p)
     turn = chunks // per
@@ -779,17 +781,18 @@
     recv = lax.all_to_all(send, "tx", split_axis=0, concat_axis=0, tiled=True)
     chunks = lmax * block // CHUNK
     wide = pixels + 3 * LANES
-    table, checks, prefix, behind, dense = pl.pallas_call(
+    table, alphas, checks, prefix, behind, dense = pl.pallas_call(
         functools.partial(forward_kernel, side),
         out_shape=(
             jax.ShapeDtypeStruct((lmax * block, LANES), BF16),
+            f32((lmax * block, pixels)),
             f32((chunks * (STEPS // SPAN), SEGS, pixels)),
             f32((SEGS, pixels)),
             f32((3, SEGS, pixels)),
             f32((6 * groups, LANES)),
         ),
         in_specs=[SMEM, SMEM, VMEM, VMEM],
-        out_specs=(VMEM,) * 5,
+        out_specs=(VMEM,) * 6,
         scratch_shapes=[
             pltpu.VMEM((LANES, wide), BF16),
             pltpu.VMEM((lmax * block, LANES), F32),
@@ -814,16 +817,16 @@
         lax.ppermute(part, "ty", [(i, (i + k) % down) for i in range(down)]) for k in range(1, down)
     ]
     stage = pl.pallas_call(
-        functools.partial(backward_kernel, side),
+        backward_kernel,
         out_shape=f32((lmax, 16, LANES)),
-        in_specs=[VMEM] * 6,
+        in_specs=[VMEM] * 7,
         out_specs=VMEM,
         scratch_shapes=[
-            pltpu.VMEM((LANES, 2 * pixels), BF16),
+            pltpu.VMEM((LANES, pixels), BF16),
             pltpu.VMEM((LANES, pixels), F32),
             pltpu.VMEM((3, SEGS, pixels), F32),
-            pltpu.VMEM((CHUNK, 2 * pixels), F32),
-            pltpu.VMEM((CHUNK, 2 * pixels), F32),
+            pltpu.VMEM((CHUNK, pixels), F32),
+            pltpu.VMEM((CHUNK, pixels), F32),
             pltpu.VMEM((SEGS, pixels), F32),
             pltpu.VMEM((CHUNK, 3 * LANES), F32),
             pltpu.VMEM((CHUNK, 3 * LANES), F32),
@@ -831,7 +834,7 @@
         ],
         compiler_params=PARAMS,
         name="backward",
-    )(table, checks, prefix, behind, slope, reduce)
+    )(table, alphas, checks, prefix, behind, slope, reduce)
     reply = pl.pallas_call(
         deliver_kernel,
         out_shape=f32((across, depth, block)),

time: 84 us -> 91.8 us (1.093)
  Pallas kernels: 29.8 us -> 37.9 us
    pallas_call x1, Pallas kernels: 12.2 us -> 19 us  [per_device(): pl.pallas_call(backward_kernel, out_shape=f32((lmax, 16, LANES)), in_spec...]
    pallas_call x1, Pallas kernels: 7.4 us -> 8.61 us  [per_device(): pl.pallas_call(functools.partial(forward_kernel, side), out_shape=(jax.Sh...]
  transfers between devices with their start and end apart: 9 -> 9, of which waited for: 5 -> 5; matrix products, arithmetic and copies ran while one was open for 0% -> 0% of each run, Pallas kernels for 15% -> 22%
where the time goes in v1:
time: 91.8 us; the launch traced here: 91.3 us
  Pallas kernels  37.9 us (41%)
  starting transfers between devices  22.5 us (25%)
  waiting for transfers between devices  16.5 us (18%)
  blocking collectives  11.1 us (12%)
  local copies, waits for them, and re-layouts  1.92 us (2%)
  between operations  1.4 us (2%)
    pallas_call x1, Pallas kernels, per_device(): pl.pallas_call(backward_kernel, out_shape=f32((lmax, 16, LANES)), in_spec...  19 us
    all_to_all x1, blocking collectives, per_device(): got = lax.all_to_all(reply, 'tx', split_axis=0, concat_axis=0, tiled=True)  11.1 us
    pallas_call x1, Pallas kernels, per_device(): pl.pallas_call(functools.partial(forward_kernel, side), out_shape=(jax.Sh...  8.61 us
    all_to_all x1, starting transfers between devices, per_device(): lax.all_to_all(request, 'tx', split_axis=0, concat_axis=0, tiled=True)  7.25 us
    all_to_all x1, waiting for transfers between devices, per_device(): recv = lax.all_to_all(send, 'tx', split_axis=0, concat_axis=0, tiled=True)  7.19 us
    ppermute x2, starting transfers between devices, shifted(): lax.ppermute(x, axis, up)  5.16 us
    ppermute x3, starting transfers between devices, per_device(): lax.ppermute(part, 'ty', [(i, (i + k) % down) for i in range(down)])  4.19 us
    ppermute x2, waiting for transfers between devices, shifted(): lax.ppermute(x, axis, [(j, i) for i, j in up])  4.17 us
  transfers between devices with their start and end apart: 9, of which 5 were waited for; matrix products, arithmetic and copies ran while one was open for 0% of the time, Pallas kernels for 22%

profile of v1, /device:TPU:0, one launch (start us, length us, event | category | flops | bytes accessed | tf_op | source)
XLA Modules:
  0.0 91.3 jit_solution(4890154081891858225)
XLA Ops:
  1.3 1.8 %request.1 = (s32[8,1,128]{2,1,0:T(1,128)}, s32[24]{0:T(128)}) custom-call(s32[1,1,24]{2,1,0:T(1,128)} %lists.1, s32[1,1]{1,0:T(1,128)S(6)} %copy.10.count, s32[3072]{0:T(1024)} %order.1), custom_call_target="tpu_custom_call" | custom-call | tf_op jit(solution)/shard_map/request/pallas_call | solution.py:755
  3.1 7.3 %all-to-all-start = ((s32[8,1,128]{2,1,0:T(1,128)}), s32[8,1,128]{2,1,0:T(1,128)S(1)}, u32[]{:S(2)}, u32[]{:S(2)}) async-start(s32[8,1,128]{2,1,0:T(1,128)} %get-tuple-element.14), calls=%async_computation | async-start | bytes 8192 | tf_op jit(solution)/shard_map/all_to_all | solution.py:763
  10.4 1.8 %copy-done = f32[96,59,128]{2,0,1:T(8,128)S(1)} copy-done((f32[96,59,128]{2,0,1:T(8,128)S(1)}, f32[96,59,128]{2,0,1:T(8,128)}, u32[]{:S(2)}) %copy-start) | copy-done | bytes 2899992
  12.2 0.6 project.1.projected
  12.8 3.9 %all-to-all-done.asked = s32[8,1,128]{2,1,0:T(1,128)S(1)} async-done(((s32[8,1,128]{2,1,0:T(1,128)}), s32[8,1,128]{2,1,0:T(1,128)S(1)}, u32[]{:S(2)}, u32[]{:S(2)}) %all-to-all-start) | async-done | bytes 4128 | tf_op jit(solution)/shard_map/all_to_all | solution.py:763
  16.8 1.4 %serve.1 = f32[8,32,128]{2,1,0:T(8,128)} custom-call(s32[8,1,128]{2,1,0:T(1,128)S(1)} %all-to-all-done.asked, f32[9,96,128]{2,1,0:T(8,128)S(1)} %project.1.projected), custom_call_target="tpu_custom_call" | custom-call | tf_op jit(solution)/shard_map/serve/pallas_call | solution.py:772
  18.2 3.4 %all-to-all-start.1 = ((f32[8,32,128]{2,1,0:T(8,128)}), f32[8,32,128]{2,1,0:T(8,128)S(1)}, u32[]{:S(2)}, u32[]{:S(2)}) async-start(f32[8,32,128]{2,1,0:T(8,128)} %serve.1), calls=%async_computation.1 | async-start | bytes 262144 | tf_op jit(solution)/shard_map/all_to_all | solution.py:781
  21.7 7.2 %all-to-all-done.1.recv = f32[8,32,128]{2,1,0:T(8,128)S(1)} async-done(((f32[8,32,128]{2,1,0:T(8,128)}), f32[8,32,128]{2,1,0:T(8,128)S(1)}, u32[]{:S(2)}, u32[]{:S(2)}) %all-to-all-start.1) | async-done | bytes 131104 | tf_op jit(solution)/shard_map/all_to_all | solution.py:781
  28.9 8.6 %forward.1 = (bf16[3072,128]{1,0:T(8,128)(2,1)S(1)}, f32[3072,1024]{1,0:T(8,128)S(1)}, f32[96,8,1024]{2,1,0:T(8,128)S(1)}, f32[8,1024]{1,0:T(8,128)S(1)}, f32[3,...) custom-call(s32[24]{0:T(128)S(1)} %copy-done.3, s32[1,1]{1,0:T(1,128)S(6)} %copy.10.count, ...), custom_call_target="tpu_custom_call" | custom-call | tf_op jit(solution)/shard_map/forward/pallas_call | solution.py:784
  37.5 2.1 %collective-permute-start = (f32[48,128]{1,0:T(8,128)S(1)}, f32[48,128]{1,0:T(8,128)S(1)}, u32[]{:S(2)}, u32[]{:S(2)}) collective-permute-start(f32[48,128]{1,0:T(8,128)S(1)} %get-tuple-element.21.refs_2_), channel_id=1, source_target_pairs={{0,1},{1,2},{2,3},{3,4},{4,5},{5,6},{6,7},{8,9},{9,10},{10,11},{11... | collective-permute-start | bytes 73736 | tf_op jit(solution)/shard_map/ppermute | solution.py:735
  39.6 1.3 %collective-permute-start.1 = (f32[48,128]{1,0:T(8,128)S(1)}, f32[48,128]{1,0:T(8,128)S(1)}, u32[]{:S(2)}, u32[]{:S(2)}) collective-permute-start(f32[48,128]{1,0:T(8,128)S(1)} %get-tuple-element.21.refs_2_), channel_id=1, source_target_pairs={{1,0},{2,1},{3,2},{4,3},{5,4},{6,5},{7,6},{9,8},{10,9},{11,10},{12... | collective-permute-start | bytes 73736 | tf_op jit(solution)/shard_map/ppermute | solution.py:735
  40.9 0.2 collective-permute-done.refs_1_
  41.2 4.2 %collective-permute-done.1.refs_3_ = f32[48,128]{1,0:T(8,128)S(1)} collective-permute-done((f32[48,128]{1,0:T(8,128)S(1)}, f32[48,128]{1,0:T(8,128)S(1)}, u32[]{:S(2)}, u32[]{:S(2)}) %collective-permute-start.1) | collective-permute-done | bytes 24608 | tf_op jit(solution)/shard_map/ppermute | solution.py:735
  45.4 1.3 %collective-permute-start.3 = (f32[144,128]{1,0:T(8,128)S(1)}, f32[144,128]{1,0:T(8,128)S(1)}, u32[]{:S(2)}, u32[]{:S(2)}) collective-permute-start(f32[144,128]{1,0:T(8,128)S(1)} %constant_dynamic-update-slice_fusion), channel_id=1, source_target_pairs={{8,0},{16,8},{24,16},{9,1},{17,9},{25,17},{10,2},{18,10},{26,18},{... | collective-permute-start | bytes 221192 | tf_op jit(solution)/shard_map/ppermute | solution.py:735
  46.6 3.0 %collective-permute-start.2 = (f32[144,128]{1,0:T(8,128)S(1)}, f32[144,128]{1,0:T(8,128)S(1)}, u32[]{:S(2)}, u32[]{:S(2)}) collective-permute-start(f32[144,128]{1,0:T(8,128)S(1)} %constant_dynamic-update-slice_fusion), channel_id=1, source_target_pairs={{0,8},{8,16},{16,24},{1,9},{9,17},{17,25},{2,10},{10,18},{18,26},{... | collective-permute-start | bytes 221192 | tf_op jit(solution)/shard_map/ppermute | solution.py:735
  49.7 0.9 collective-permute-done.2.refs_0_
  50.6 2.6 %score.1 = (f32[24,128]{1,0:T(8,128)S(1)}, f32[8,128]{1,0:T(8,128)S(1)}) custom-call(f32[144,128]{1,0:T(8,128)S(1)} %collective-permute-done.2.refs_0_, f32[48,128]{1,0:T(8,128)S(1)} %collective-permute-done.refs_1_, f32[48,128]{1,0:T(8,128)S(1)} %get-tuple-element.21.refs_2_, f32[48,128]{1,0:T(8,128)S(1)} %collective-permute-done.1.refs_3_, ...), custom_call_target="tpu_custom_call" | custom-call | tf_op jit(solution)/shard_map/score/pallas_call | solution.py:808
  53.2 1.5 %collective-permute-start.6 = (f32[8,128]{1,0:T(8,128)S(1)}, f32[8,128]{1,0:T(8,128)S(1)}, u32[]{:S(2)}, u32[]{:S(2)}) collective-permute-start(f32[8,128]{1,0:T(8,128)S(1)} %get-tuple-element.23.refs_0_), channel_id=1, source_target_pairs={{0,24},{8,0},{16,8},{24,16},{1,25},{9,1},{17,9},{25,17},{2,26},{10... | collective-permute-start | bytes 12296 | tf_op jit(solution)/shard_map/ppermute | solution.py:817
  54.7 2.5 %collective-permute-start.5 = (f32[8,128]{1,0:T(8,128)S(1)}, f32[8,128]{1,0:T(8,128)S(1)}, u32[]{:S(2)}, u32[]{:S(2)}) collective-permute-start(f32[8,128]{1,0:T(8,128)S(1)} %get-tuple-element.23.refs_0_), channel_id=1, source_target_pairs={{0,16},{8,24},{16,0},{24,8},{1,17},{9,25},{17,1},{25,9},{2,18},{10... | collective-permute-start | bytes 12296 | tf_op jit(solution)/shard_map/ppermute | solution.py:817
  57.2 0.2 collective-permute-start.4
  57.4 19.0 %backward.1.stage = f32[24,16,128]{2,1,0:T(8,128)S(1)} custom-call(bf16[3072,128]{1,0:T(8,128)(2,1)S(1)} %get-tuple-element.16.table, f32[3072,1024]{1,0:T(8,128)S(1)} %get-tuple-element.17.alphas, f32[96,8,1024]{2,1,0:T(8,128)S(1)} %get-tuple-element.18.checks, f32[8,1024]{1,0:T(8,128)S(1)} %get-tuple-element.19.prefix, ...), custom_call_target="tpu_custom_call" | custom-call | tf_op jit(solution)/shard_map/backward/pallas_call | solution.py:819
  76.5 0.7 deliver.1
  77.2 11.1 %all_to_all.15.got = f32[8,32,128]{2,1,0:T(8,128)S(1)} all-to-all(f32[8,32,128]{2,1,0:T(8,128)S(1)} %deliver.1), channel_id=1, replica_groups=mesh['ty'=4,'tx'=8] {'tx'}, dimensions={0} | all-to-all | bytes 262144 | tf_op jit(solution)/shard_map/all_to_all | solution.py:846
  88.3 3.0 %gather.1 = (f32[59,96,128]{2,1,0:T(8,128)}, f32[1]{0:T(128)}) custom-call(s32[8,1,128]{2,1,0:T(1,128)S(1)} %all-to-all-done.asked, f32[8,32,128]{2,1,0:T(8,128)S(1)} %all_to_all.15.got, f32[59,96,128]{2,1,0:T(8,128)S(1)} %bitcast.4), custom_call_target="tpu_custom_call" | custom-call | tf_op jit(solution)/shard_map/gather/pallas_call | solution.py:847
  (17 shorter events, 0.1 us)
Async XLA Ops:
  3.1 25.8 %copy-start.3 = (s32[24]{0:T(128)S(1)}, s32[24]{0:T(128)}, u32[]{:S(2)}) copy-start(s32[24]{0:T(128)} %get-tuple-element.15.slot) | copy-start | bytes 292
  3.1 13.6 %all-to-all-start = ((s32[8,1,128]{2,1,0:T(1,128)}), s32[8,1,128]{2,1,0:T(1,128)S(1)}, u32[]{:S(2)}, u32[]{:S(2)}) async-start(s32[8,1,128]{2,1,0:T(1,128)} %get-tuple-element.14), calls=%async_computation | async-start | bytes 8192 | tf_op jit(solution)/shard_map/all_to_all | solution.py:763
  10.4 1.8 %copy-start = (f32[96,59,128]{2,0,1:T(8,128)S(1)}, f32[96,59,128]{2,0,1:T(8,128)}, u32[]{:S(2)}) copy-start(f32[96,59,128]{2,0,1:T(8,128)} %param.6) | copy-start | bytes 8699908
  12.2 9.4 %copy-start.4 = (f32[3,32,32]{2,1,0:T(8,128)S(1)}, f32[3,32,32]{2,1,0:T(8,128)}, u32[]{:S(2)}) copy-start(f32[3,32,32]{2,1,0:T(8,128)} %param.10) | copy-start | bytes 36868
  12.2 45.2 %copy-start.2 = (bf16[384,128]{1,0:T(8,128)(2,1)S(1)}, bf16[384,128]{1,0:T(8,128)(2,1)}, u32[]{:S(2)}) copy-start(bf16[384,128]{1,0:T(8,128)(2,1)} %constant.2.clone.reduce) | copy-start | bytes 294916
  18.2 10.7 %all-to-all-start.1 = ((f32[8,32,128]{2,1,0:T(8,128)}), f32[8,32,128]{2,1,0:T(8,128)S(1)}, u32[]{:S(2)}, u32[]{:S(2)}) async-start(f32[8,32,128]{2,1,0:T(8,128)} %serve.1), calls=%async_computation.1 | async-start | bytes 262144 | tf_op jit(solution)/shard_map/all_to_all | solution.py:781
  37.5 3.7 %collective-permute-start = (f32[48,128]{1,0:T(8,128)S(1)}, f32[48,128]{1,0:T(8,128)S(1)}, u32[]{:S(2)}, u32[]{:S(2)}) collective-permute-start(f32[48,128]{1,0:T(8,128)S(1)} %get-tuple-element.21.refs_2_), channel_id=1, source_target_pairs={{0,1},{1,2},{2,3},{3,4},{4,5},{5,6},{6,7},{8,9},{9,10},{10,11},{11... | collective-permute-start | bytes 73736 | tf_op jit(solution)/shard_map/ppermute | solution.py:735
  39.6 5.7 %collective-permute-start.1 = (f32[48,128]{1,0:T(8,128)S(1)}, f32[48,128]{1,0:T(8,128)S(1)}, u32[]{:S(2)}, u32[]{:S(2)}) collective-permute-start(f32[48,128]{1,0:T(8,128)S(1)} %get-tuple-element.21.refs_2_), channel_id=1, source_target_pairs={{1,0},{2,1},{3,2},{4,3},{5,4},{6,5},{7,6},{9,8},{10,9},{11,10},{12... | collective-permute-start | bytes 73736 | tf_op jit(solution)/shard_map/ppermute | solution.py:735
  45.4 4.3 %collective-permute-start.3 = (f32[144,128]{1,0:T(8,128)S(1)}, f32[144,128]{1,0:T(8,128)S(1)}, u32[]{:S(2)}, u32[]{:S(2)}) collective-permute-start(f32[144,128]{1,0:T(8,128)S(1)} %constant_dynamic-update-slice_fusion), channel_id=1, source_target_pairs={{8,0},{16,8},{24,16},{9,1},{17,9},{25,17},{10,2},{18,10},{26,18},{... | collective-permute-start | bytes 221192 | tf_op jit(solution)/shard_map/ppermute | solution.py:735
  46.6 3.9 %collective-permute-start.2 = (f32[144,128]{1,0:T(8,128)S(1)}, f32[144,128]{1,0:T(8,128)S(1)}, u32[]{:S(2)}, u32[]{:S(2)}) collective-permute-start(f32[144,128]{1,0:T(8,128)S(1)} %constant_dynamic-update-slice_fusion), channel_id=1, source_target_pairs={{0,8},{8,16},{16,24},{1,9},{9,17},{17,25},{2,10},{10,18},{18,26},{... | collective-permute-start | bytes 221192 | tf_op jit(solution)/shard_map/ppermute | solution.py:735
  53.2 23.2 %collective-permute-start.6 = (f32[8,128]{1,0:T(8,128)S(1)}, f32[8,128]{1,0:T(8,128)S(1)}, u32[]{:S(2)}, u32[]{:S(2)}) collective-permute-start(f32[8,128]{1,0:T(8,128)S(1)} %get-tuple-element.23.refs_0_), channel_id=1, source_target_pairs={{0,24},{8,0},{16,8},{24,16},{1,25},{9,1},{17,9},{25,17},{2,26},{10... | collective-permute-start | bytes 12296 | tf_op jit(solution)/shard_map/ppermute | solution.py:817
  54.7 21.7 %collective-permute-start.5 = (f32[8,128]{1,0:T(8,128)S(1)}, f32[8,128]{1,0:T(8,128)S(1)}, u32[]{:S(2)}, u32[]{:S(2)}) collective-permute-start(f32[8,128]{1,0:T(8,128)S(1)} %get-tuple-element.23.refs_0_), channel_id=1, source_target_pairs={{0,16},{8,24},{16,0},{24,8},{1,17},{9,25},{17,1},{25,9},{2,18},{10... | collective-permute-start | bytes 12296 | tf_op jit(solution)/shard_map/ppermute | solution.py:817
  57.2 19.2 %collective-permute-start.4 = (f32[8,128]{1,0:T(8,128)S(1)}, f32[8,128]{1,0:T(8,128)S(1)}, u32[]{:S(2)}, u32[]{:S(2)}) collective-permute-start(f32[8,128]{1,0:T(8,128)S(1)} %get-tuple-element.23.refs_0_), channel_id=1, source_target_pairs={{0,8},{8,16},{16,24},{24,0},{1,9},{9,17},{17,25},{25,1},{2,10},{10... | collective-permute-start | bytes 12296 | tf_op jit(solution)/shard_map/ppermute | solution.py:817
  57.4 30.9 %copy-start.1 = (f32[96,59,128]{2,0,1:T(8,128)S(1)}, f32[96,59,128]{2,0,1:T(8,128)}, u32[]{:S(2)}) copy-start(f32[96,59,128]{2,0,1:T(8,128)} %param.6) | copy-start | bytes 8699908
